TPU v7x, 512 devices: a whole 4x8x8 slice. The times are simulated.
512 devices in a mesh: pipe: 8 (over z), seq: 64 (over x, y, core).
Axes of the slice: x: 4, y: 8, z: 8, core: 2. Of those that a mesh axis runs over, the one named last changes fastest.
Arguments:
- activations: bfloat16 [8, 8192, 2048], P('pipe', 'seq'), may hold values from -6 to 6
- norm_gain: float32 [8, 2048], P('pipe'), may hold values from 0.1 to 1.9
- conv_kernels: float32 [8, 3, 4, 2048], P('pipe'), may hold values from -3 to 3
- out_gain: float32 [8, 2048], P('pipe'), may hold values from 0.1 to 1.9
Outputs:
- handed: bfloat16 [8, 8192, 2048], P('pipe', 'seq')
All inputs are finite; a program needn't handle non-finite values.
Results may differ from a plain program's by a relative error of at most 0.0052.
Values may be sent and summed in bfloat16 or wider, within the bound.
A program may use at most 192 MiB of HBM per device.

v0:
```python
import jax
import jax.numpy as jnp
from jax import lax
from jax.sharding import PartitionSpec as P

DH = 128


def from_behind(value, axis, by):
    count = lax.axis_size(axis)
    pairs = [(i, i + by) for i in range(count) if 0 <= i + by < count]
    return lax.ppermute(value, axis, pairs)


def carried_in(value, axis, join, neutral):
    place = lax.axis_index(axis)
    gathered = lax.all_gather(value.astype(jnp.bfloat16), axis)
    state = jnp.zeros_like(value) + jnp.asarray(neutral, value.dtype)

    def one(hop, state):
        return join(state, lax.dynamic_index_in_dim(gathered, hop, 0, False).astype(value.dtype))

    return lax.fori_loop(0, place, one, state)


def from_behind_2(value, axis, by):
    count = lax.axis_size(axis)
    return lax.ppermute(value, axis, [(i, (i + by) % count) for i in range(count)])


def normalize(row_block, row_gain):
    row_values = row_block.astype(jnp.float32)
    factor = lax.rsqrt(jnp.mean(row_values * row_values, axis=-1, keepdims=True) + 1e-06)
    return (row_values * factor * row_gain).astype(jnp.bfloat16)


def convolve(padded, kernel, kernel_width, tok_count):
    summed = jnp.zeros((tok_count, padded.shape[1]), jnp.float32)
    for offset in range(kernel_width):
        first_row = kernel_width - 1 - offset
        summed = summed + kernel[offset] * padded[first_row : first_row + tok_count].astype(
            jnp.float32
        )
    return summed


def split_heads(matrix):
    tok_count = matrix.shape[0]
    return matrix.reshape(tok_count, matrix.shape[1] // DH, DH).transpose(1, 0, 2)


def own_state(key_rows, value_rows):
    return jnp.einsum("htd,hte->hde", key_rows, value_rows, preferred_element_type=jnp.float32)


def add_states(earlier, latest):
    return earlier + latest


def finish(queries, key_rows, value_rows, prefix, residual, row_gain):
    carried = jnp.einsum(
        "htd,hde->hte", queries.astype(jnp.float32), prefix, precision=lax.Precision.HIGHEST
    )
    tok_count = queries.shape[1]
    causal = jnp.tril(jnp.ones((tok_count, tok_count), dtype=bool))

    def one_head(pieces):
        query_h, key_h, value_h = pieces
        scores = jnp.dot(query_h, key_h.T, preferred_element_type=jnp.float32)
        weights = jnp.where(causal, scores, 0.0).astype(jnp.bfloat16)
        return jnp.dot(weights, value_h, preferred_element_type=jnp.float32)

    within = lax.map(one_head, (queries, key_rows, value_rows))
    mixed_out = carried + within
    scaled = mixed_out * lax.rsqrt(jnp.mean(mixed_out * mixed_out, axis=-1, keepdims=True) + 1e-06)
    merged = scaled.transpose(1, 0, 2).reshape(tok_count, -1)
    return (residual.astype(jnp.float32) + merged * row_gain).astype(jnp.bfloat16)


def body(activations, norm_gain, conv_kernels, out_gain):
    section_rows = activations[0]
    gain_in = norm_gain[0]
    gain_out = out_gain[0]
    kernels = conv_kernels[0]
    kernel_width = kernels.shape[1]
    tok_count = section_rows.shape[0]
    normed = normalize(section_rows, gain_in)
    first_row = tok_count - (kernel_width - 1)
    rim_rows = from_behind(normed[first_row:], "seq", 1)
    padded = jnp.concatenate([rim_rows, normed], 0)
    query_all = (jax.nn.elu(convolve(padded, kernels[0], kernel_width, tok_count)) + 1.0).astype(
        jnp.bfloat16
    )
    key_all = (jax.nn.elu(convolve(padded, kernels[1], kernel_width, tok_count)) + 1.0).astype(
        jnp.bfloat16
    )
    value_all = convolve(padded, kernels[2], kernel_width, tok_count).astype(jnp.bfloat16)
    queries = split_heads(query_all)
    key_rows = split_heads(key_all)
    value_rows = split_heads(value_all)
    state_all = own_state(key_rows, value_rows)
    prefix = carried_in(state_all, "seq", add_states, jnp.zeros_like(state_all))
    result = finish(queries, key_rows, value_rows, prefix, section_rows, gain_out)
    handed = from_behind_2(result, "pipe", 1)
    return handed[None]


def solution(mesh):
    placed = (P("pipe", "seq", None), P("pipe", None), P("pipe", None, None, None), P("pipe", None))
    return jax.shard_map(
        body, mesh=mesh, in_specs=placed, out_specs=P("pipe", "seq", None), check_vma=False
    )
```

profile of v0, /device:TPU:63, one launch (start us, length us, event | category | flops | bytes accessed | tf_op | source)
XLA Modules:
  0.0 277.8 jit_solution(12244406102247552749)
XLA Ops:
  6.5 1.3 fusion.28
  9.1 1.3 collective-permute-start
  16.0 14.9 %while.22 = (s32[]{:T(128)}, f32[16,128,128]{1,2,0:T(8,128)}, bf16[16,128,128]{2,1,0:T(8,128)(2,1)S(1)}, bf16[16,128,128]{2,1,0:T(8,128)(2,1)S(1)}, bf16[16,128,128]{2,1,0:T(8,128)(2,1)S(1)}, /*index=5*/s32[]{:T(128)}) while((s32[]{:T(128)}, f32[16,128,128]{1,2,0:T(8,128)}, bf16[16,128,128]{2,1,0:T(8,128)(2,1)S(1)}, ...), condition=%wide.region_4.5_spmd.clone, body=%wide.region_3.4_spmd.clone.sunk | while | flops 8437762 | bytes 165965 | solution.py:73
  30.9 135.9 %all-gather.3.cloned.1.call-done = bf16[1024,128,128]{2,1,0:T(8,128)(2,1)} async-done(((bf16[16,128,128]{2,1,0:T(8,128)(2,1)}), bf16[1024,128,128]{2,1,0:T(8,128)(2,1)}) %all-gather.3.cloned.1.call-update) | async-done | bytes 33554448 | tf_op jit(solution)/shard_map/all_gather | solution.py:17
  166.9 82.5 %while.21 = (s32[]{:T(128)}, f32[16,128,128]{2,1,0:T(8,128)S(1)}, s32[]{:T(128)}, bf16[64,16,128,128]{3,2,1,0:T(8,128)(2,1)}, s32[]{:T(128)}, /*index=5*/s32[]{:T(128)}, s32[]{:T(128)}) while((s32[]{:T(128)}, f32[16,128,128]{2,1,0:T(8,128)S(1)}, s32[]{:T(128)}, bf16[64,16,128,128]{3,2,1,0:T(8,128)(2,1)}, s32[]{:T(128)}, /*index=5*/s32[]{:T(128)}, ...), condition=%wide.region_2.3_spmd, body=%wide.region_1.2_spmd.sunk | while | flops 524293 | bytes 2621563 | solution.py:23
  166.9 1.3 convert_add_fusion.3
  168.2 1.3 convert_add_fusion.3
  169.5 1.3 convert_add_fusion.3
  170.8 1.3 convert_add_fusion.3
  172.1 1.3 convert_add_fusion.3
  173.4 1.3 convert_add_fusion.3
  174.8 1.3 convert_add_fusion.3
  176.1 1.3 convert_add_fusion.3
  177.4 1.3 convert_add_fusion.3
  178.7 1.3 convert_add_fusion.3
  180.0 1.3 convert_add_fusion.3
  181.3 1.3 convert_add_fusion.3
  182.6 1.3 convert_add_fusion.3
  183.9 1.3 convert_add_fusion.3
  185.2 1.3 convert_add_fusion.3
  186.5 1.3 convert_add_fusion.3
  187.9 1.3 convert_add_fusion.3
  189.2 1.3 convert_add_fusion.3
  190.5 1.3 convert_add_fusion.3
  191.8 1.3 convert_add_fusion.3
  193.1 1.3 convert_add_fusion.3
  194.4 1.3 convert_add_fusion.3
  195.7 1.3 convert_add_fusion.3
  197.0 1.3 convert_add_fusion.3
  198.3 1.3 convert_add_fusion.3
  199.6 1.3 convert_add_fusion.3
  201.0 1.3 convert_add_fusion.3
  202.3 1.3 convert_add_fusion.3
  203.6 1.3 convert_add_fusion.3
  204.9 1.3 convert_add_fusion.3
  206.2 1.3 convert_add_fusion.3
  207.5 1.3 convert_add_fusion.3
  208.8 1.3 convert_add_fusion.3
  210.1 1.3 convert_add_fusion.3
  211.4 1.3 convert_add_fusion.3
  212.7 1.3 convert_add_fusion.3
  214.1 1.3 convert_add_fusion.3
  215.4 1.3 convert_add_fusion.3
  216.7 1.3 convert_add_fusion.3
  218.0 1.3 convert_add_fusion.3
  249.4 3.2 %multiply_reduce_fusion = (f32[16,128]{1,0:T(8,128)S(1)}, f32[16,128,128]{1,2,0:T(8,128)S(1)}) fusion(f32[16,128,128]{1,2,0:T(8,128)} %get-tuple-element.61, f32[16,128,128]{2,1,0:T(8,128)S(1)} %get-tuple-element.60, bf16[128,2048]{1,0:T(8,128)(2,1)S(1)} %fusion.30, bf16[3,2048]{1,0:T(4,128)(2,1)S(1)} %collective-permute-done, f32[2048]{0:T(1024)S(1)} %bitcast.94, ...), kind=kOutput, calls=%fused_computation.55 | convolution fusion | flops 409991168 | bytes 3723264 | tf_op jit(solution)/shard_map/htd,hde->hte/dot_general | solution.py:61
  253.2 3.3 %collective-permute-start.1 = (bf16[128,2048]{1,0:T(8,128)(2,1)S(1)}, bf16[128,2048]{1,0:T(8,128)(2,1)S(1)}, u32[]{:S(2)}, u32[]{:S(2)}) collective-permute-start(bf16[128,2048]{1,0:T(8,128)(2,1)S(1)} %fusion.31), channel_id=1, source_target_pairs={{0,64},{64,128},{128,192},{192,256},{256,320},{320,384},{384,448},... | collective-permute-start | bytes 1572872 | tf_op jit(solution)/shard_map/ppermute | solution.py:28
  256.5 13.6 %collective-permute-done.1 = bf16[128,2048]{1,0:T(8,128)(2,1)S(1)} collective-permute-done((bf16[128,2048]{1,0:T(8,128)(2,1)S(1)}, bf16[128,2048]{1,0:T(8,128)(2,1)S(1)}, u32[]{:S(2)}, u32[]{:S(2)}) %collective-permute-start.1) | collective-permute-done | bytes 524320 | tf_op jit(solution)/shard_map/ppermute | solution.py:28
  (62 shorter events, 52.8 us)
Async XLA Ops:
  6.5 246.5 %copy-start = (bf16[1,128,2048]{2,1,0:T(8,128)(2,1)S(1)}, bf16[1,128,2048]{2,1,0:T(8,128)(2,1)}, u32[]{:S(2)}) copy-start(bf16[1,128,2048]{2,1,0:T(8,128)(2,1)} %param.8) | copy-start | bytes 1572868
  6.5 246.5 %copy-start.1 = (f32[1,2048]{1,0:T(1,128)S(1)}, f32[1,2048]{1,0:T(1,128)}, u32[]{:S(2)}) copy-start(f32[1,2048]{1,0:T(1,128)} %param.11) | copy-start | bytes 24580
  6.5 160.2 %all-gather.3.cloned.1.call-start = ((), (), s32[]{:S(2)}) async-start(), calls=%async_computation | async-start | bytes 34078720 | tf_op jit(solution)/shard_map/all_gather | solution.py:17
  9.1 3.3 %collective-permute-start = (bf16[3,2048]{1,0:T(4,128)(2,1)S(1)}, bf16[3,2048]{1,0:T(4,128)(2,1)S(1)}, u32[]{:S(2)}, u32[]{:S(2)}) collective-permute-start(bf16[3,2048]{1,0:T(4,128)(2,1)S(1)} %slice.100), channel_id=1, source_target_pairs={{0,1},{1,2},{2,3},{3,4},{4,5},{5,6},{6,7},{7,8},{8,9},{9,10},{10,1... | collective-permute-start | bytes 36872 | tf_op jit(solution)/shard_map/ppermute | solution.py:12
  253.2 16.9 %collective-permute-start.1 = (bf16[128,2048]{1,0:T(8,128)(2,1)S(1)}, bf16[128,2048]{1,0:T(8,128)(2,1)S(1)}, u32[]{:S(2)}, u32[]{:S(2)}) collective-permute-start(bf16[128,2048]{1,0:T(8,128)(2,1)S(1)} %fusion.31), channel_id=1, source_target_pairs={{0,64},{64,128},{128,192},{192,256},{256,320},{320,384},{384,448},... | collective-permute-start | bytes 1572872 | tf_op jit(solution)/shard_map/ppermute | solution.py:28
Sparse Core Ops, SparseCore 0:
  15.0 151.7 all-gather.2
where the time goes:
time: 281 us; the launch traced here: 278 us
  waiting for transfers between devices  150 us (53%)
  other arithmetic  86.1 us (31%)
  matrix products  19.2 us (7%)
  between operations  13.5 us (5%)
  starting transfers between devices  4.57 us (2%)
    all_gather x1, waiting for transfers between devices, carried_in(): gathered = lax.all_gather(value.astype(jnp.bfloat16), axis)  136 us
    add x63, other arithmetic, add_states(): return earlier + latest  81.1 us
    dot_general x16, matrix products, one_head(): return jnp.dot(weights, value_h, preferred_element_type=jnp.float32)  14.9 us
    ppermute x1, waiting for transfers between devices, from_behind_2(): lax.ppermute(value, axis, [(i, (i + by) % count) for i in range(count)])  13.6 us
  transfers between devices with their start and end apart: 3, of which 3 were waited for; matrix products, arithmetic and copies ran while one was open for 6% of the time, Pallas kernels for 0%

commit v1 on v0

v1 whole, which is shorter than its diff:
```python
import functools

import jax
import jax.numpy as jnp
from jax import lax
from jax.experimental import pallas as pl
from jax.experimental.pallas import tpu as pltpu
from jax.sharding import PartitionSpec as P

DH = 128
HALO = 16
MESH = pl.DeviceIdType.MESH
F32 = jnp.float32
BF16 = jnp.bfloat16


def lanes(start, size):
    return pl.ds(pl.multiple_of(start, DH), size)


def kernel(
    n_pipe, n_chip, tok, heads,
    act, ngain, conv, ogain, out,
    own, xbuf, fbuf, pconv, pngain, pogain, halo, hsend, nbuf,
    qbuf, kbuf, vbuf, within, tsend, trecv, psend, pbuf, rbuf,
    load_sem, xs_sem, xr_sem, fs_sem, fr_sem, ps_sem, pr_sem, hs_sem, hr_sem,
    ts_sem, tr_sem, qs_sem, qr_sem, rs_sem, rr_sem,
):
    wide = heads * DH
    rows = 2 * tok
    part = wide // n_chip
    width = 4 * wide
    pipe = lax.axis_index("pipe")
    seq = lax.axis_index("seq")
    core = seq % 2
    chip = seq // 2
    ahead = (pipe + 1) % n_pipe
    behind = (pipe + n_pipe - 1) % n_pipe
    peer = seq + 1 - 2 * core

    def a_cols(which):
        return which * (2 * wide)

    def b_cols(which):
        return which * (2 * wide) + wide

    def local(src, dst, sem):
        return pltpu.make_async_copy(src, dst, sem)

    def remote(src, dst, send, recv, to_pipe, to_seq):
        return pltpu.make_async_remote_copy(
            src_ref=src, dst_ref=dst, send_sem=send, recv_sem=recv,
            device_id=(to_pipe, to_seq), device_id_type=MESH,
        )

    barrier = pltpu.get_barrier_semaphore()

    def greet(step, carry):
        other = 2 * ((chip + step) % n_chip) + core
        pl.semaphore_signal(barrier, inc=1, device_id=(pipe, other), device_id_type=MESH)
        return carry

    pl.semaphore_signal(barrier, inc=1, device_id=(pipe, peer), device_id_type=MESH)
    for which in range(2):
        pl.semaphore_signal(
            barrier, inc=1, device_id=(behind, 2 * chip + which), device_id_type=MESH
        )
    lax.fori_loop(1, n_chip, greet, 0)

    loads = [
        local(act, own, load_sem.at[0]),
        local(act.at[:, lanes(a_cols(core), wide)], xbuf.at[0, core], load_sem.at[1]),
        local(conv.at[:, :, lanes(a_cols(core), wide)], pconv.at[0], load_sem.at[2]),
        local(ngain.at[:, lanes(a_cols(core), wide)], pngain.at[0], load_sem.at[3]),
        local(ogain.at[:, lanes(a_cols(core), wide)], pogain.at[0], load_sem.at[4]),
    ]
    for load in loads:
        load.start()
    pl.semaphore_wait(barrier, n_chip + 2)

    x_copies = [
        remote(
            act.at[:, lanes(a_cols(1 - core), wide)], xbuf.at[0, core],
            xs_sem.at[0], xr_sem.at[0], pipe, peer,
        )
    ]
    for which in range(2):
        x_copies.append(
            remote(
                act.at[:, lanes(b_cols(which), wide)], xbuf.at[1, core],
                xs_sem.at[1 + which], xr_sem.at[1 + core], ahead, 2 * chip + which,
            )
        )
    p_copies = [
        remote(
            conv.at[:, :, lanes(b_cols(core), wide)], pconv.at[1],
            ps_sem.at[0], pr_sem.at[0], ahead, seq,
        ),
        remote(
            ngain.at[:, lanes(b_cols(core), wide)], pngain.at[1],
            ps_sem.at[1], pr_sem.at[1], ahead, seq,
        ),
        remote(
            ogain.at[:, lanes(b_cols(core), wide)], pogain.at[1],
            ps_sem.at[2], pr_sem.at[2], ahead, seq,
        ),
    ]
    for copy in x_copies + p_copies:
        copy.start()

    loads[0].wait()
    squares = jnp.zeros((tok, DH), F32)
    for piece in range(width // DH):
        values = own[:, piece * DH : (piece + 1) * DH].astype(F32)
        squares = squares + values * values
    mean = jnp.sum(squares, axis=-1, keepdims=True) * (1.0 / width)
    factor = jnp.broadcast_to(lax.rsqrt(mean + 1e-06), (tok, DH))
    fbuf[0, core] = factor.T[:8]
    f_copies = [
        remote(
            fbuf.at[0, core], fbuf.at[0, core], fs_sem.at[0], fr_sem.at[0], pipe, peer
        )
    ]
    for which in range(2):
        f_copies.append(
            remote(
                fbuf.at[0, core], fbuf.at[1, core],
                fs_sem.at[1 + which], fr_sem.at[1 + core], ahead, 2 * chip + which,
            )
        )
    for copy in f_copies:
        copy.start()

    def normalize(group):
        for block in range(2):
            column = jnp.broadcast_to(fbuf[group, block, 0:1, :], (tok, tok)).T

            def one(head, carry):
                cols = lanes(head * DH, DH)
                normed = (
                    xbuf[group, block, :, cols].astype(F32) * column * pngain[group, :, cols]
                ).astype(BF16)
                nbuf[group, pl.ds(HALO + block * tok, tok), cols] = normed.astype(F32)
                if block == 1:
                    hsend[group, :, cols] = normed[tok - HALO :]
                return carry

            lax.fori_loop(0, heads, one, 0)

    def h_copy(group):
        return remote(
            hsend.at[group], halo.at[group], hs_sem.at[group], hr_sem.at[group],
            pipe, 2 * ((chip + 1) % n_chip) + core,
        )

    def convolve(group, head, start, count):
        cols = lanes(head * DH, DH)
        shifted = [nbuf[group, pl.ds(HALO + start - i, count), cols] for i in range(4)]
        made = []
        for j in range(3):
            total = pconv[group, j, 0:1, cols] * shifted[0]
            for i in range(1, 4):
                total = total + pconv[group, j, i : i + 1, cols] * shifted[i]
            made.append(total)

        def positive(x):
            return jnp.where(x > 0.0, x + 1.0, jnp.exp(jnp.minimum(x, 0.0)))

        where = pl.ds(start, count)
        qbuf[group, where, cols] = positive(made[0]).astype(BF16)
        kbuf[group, where, cols] = positive(made[1]).astype(BF16)
        vbuf[group, where, cols] = made[2].astype(BF16)

    tile = tok // 2

    def to_states(group):
        normalize(group)
        h_copy(group).start()

        def later_rows(head, carry):
            for start in range(tile, rows, tile):
                convolve(group, head, start, tile)
            return carry

        lax.fori_loop(0, heads, later_rows, 0)
        h_copy(group).wait_recv()
        first = jnp.where(chip == 0, 0.0, halo[group].astype(F32))
        nbuf[group, 0:HALO, :] = first

        def first_rows(head, carry):
            cols = lanes(head * DH, DH)
            convolve(group, head, 0, tile)
            state = lax.dot_general(
                kbuf[group, :, cols], vbuf[group, :, cols], (((0,), (0,)), ((), ())),
                preferred_element_type=F32,
            )
            tsend[group, lanes(head * DH, DH), :] = state.astype(BF16)
            return carry

        lax.fori_loop(0, heads, first_rows, 0)

        def one(step, carry):
            other = (chip + step) % n_chip
            remote(
                tsend.at[group, pl.ds(pl.multiple_of(other * part, part), part)],
                trecv.at[group, chip], ts_sem.at[group], tr_sem.at[group],
                pipe, 2 * other + core,
            ).start()
            return carry

        lax.fori_loop(1, n_chip, one, 0)
        trecv[group, chip] = tsend[group, pl.ds(pl.multiple_of(chip * part, part), part), :]

    def inside(group):
        causal = lax.broadcasted_iota(jnp.int32, (rows, rows), 1) <= lax.broadcasted_iota(
            jnp.int32, (rows, rows), 0
        )

        def one(head, carry):
            cols = lanes(head * DH, DH)
            scores = lax.dot_general(
                qbuf[group, :, cols], kbuf[group, :, cols], (((1,), (1,)), ((), ())),
                preferred_element_type=F32,
            )
            weights = jnp.where(causal, scores, 0.0).astype(BF16)
            within[group, :, cols] = jnp.dot(
                weights, vbuf[group, :, cols], preferred_element_type=F32
            )
            return carry

        lax.fori_loop(0, heads, one, 0)

    def t_wait(group):
        return remote(
            psend.at[group, pl.ds(0, n_chip - 1)], trecv.at[group, pl.ds(0, n_chip - 1)],
            ts_sem.at[group], tr_sem.at[group], pipe, peer,
        )

    def q_wait(group):
        count = (n_chip - 1) * part
        return remote(
            tsend.at[group, pl.ds(0, count)], pbuf.at[group, pl.ds(0, count)],
            qs_sem.at[group], qr_sem.at[group], pipe, peer,
        )

    def prefixes(group):
        t_wait(group).wait_recv()

        def add(index, total):
            psend[group, index] = total.astype(BF16)
            return total + trecv[group, index].astype(F32)

        lax.fori_loop(0, n_chip, add, jnp.zeros((part, DH), F32))

        def one(step, carry):
            other = (chip + step) % n_chip
            remote(
                psend.at[group, other],
                pbuf.at[group, pl.ds(pl.multiple_of(chip * part, part), part)],
                qs_sem.at[group], qr_sem.at[group], pipe, 2 * other + core,
            ).start()
            return carry

        lax.fori_loop(1, n_chip, one, 0)
        pbuf[group, pl.ds(pl.multiple_of(chip * part, part), part), :] = psend[group, chip]

    def finish(group, send):
        q_wait(group).wait_recv()

        def one(head, carry):
            cols = lanes(head * DH, DH)
            mixed = within[group, :, cols] + jnp.dot(
                qbuf[group, :, cols], pbuf[group, lanes(head * DH, DH), :],
                preferred_element_type=F32,
            )
            scaled = mixed * lax.rsqrt(
                jnp.mean(mixed * mixed, axis=-1, keepdims=True) + 1e-06
            ) * pogain[group, :, cols]
            for block in range(2):
                residual = xbuf[group, block, :, cols].astype(F32)
                rbuf[group, block, :, cols] = (
                    residual + scaled[block * tok : (block + 1) * tok]
                ).astype(BF16)
            if send is not None:
                send(head)
            return carry

        lax.fori_loop(0, heads, one, 0)

    def hand(head):
        for block in range(2):
            remote(
                rbuf.at[0, block, :, lanes(head * DH, DH)],
                out.at[:, lanes(a_cols(core) + head * DH, DH)],
                rs_sem.at[block], rr_sem.at[core], ahead, 2 * chip + block,
            ).start()

    for load in loads[1:]:
        load.wait()
    x_copies[0].wait_recv()
    f_copies[0].wait_recv()
    to_states(0)
    inside(0)
    prefixes(0)

    for which in range(2):
        remote(
            xbuf.at[0, 0], xbuf.at[1, which], xs_sem.at[0], xr_sem.at[1 + which], ahead, seq
        ).wait_recv()
        remote(
            fbuf.at[0, 0], fbuf.at[1, which], fs_sem.at[0], fr_sem.at[1 + which], ahead, seq
        ).wait_recv()
    for copy in p_copies:
        copy.wait_recv()
    to_states(1)
    finish(0, hand)
    inside(1)
    prefixes(1)
    finish(1, None)
    keep = local(
        rbuf.at[1, core], out.at[:, lanes(b_cols(core), wide)], load_sem.at[0]
    )
    give = remote(
        rbuf.at[1, 1 - core], out.at[:, lanes(b_cols(core), wide)],
        rs_sem.at[2], rr_sem.at[2], pipe, peer,
    )
    keep.start()
    give.start()

    for copy in x_copies + p_copies + f_copies:
        copy.wait_send()
    for group in range(2):
        h_copy(group).wait_send()
        t_wait(group).wait_send()
        q_wait(group).wait_send()
    for which in range(2):
        handed = remote(
            rbuf.at[0, which], out.at[:, lanes(a_cols(which), wide)],
            rs_sem.at[which], rr_sem.at[which], ahead, seq,
        )
        handed.wait_send()
        handed.wait_recv()
    keep.wait()
    give.wait_send()
    give.wait_recv()


def body(activations, norm_gain, conv_kernels, out_gain):
    n_pipe = lax.axis_size("pipe")
    n_chip = lax.axis_size("seq") // 2
    _, tok, width = activations.shape
    wide = width // 4
    heads = wide // DH
    part = wide // n_chip
    rows = 2 * tok
    dma = pltpu.SemaphoreType.DMA
    handed = pl.pallas_call(
        functools.partial(kernel, n_pipe, n_chip, tok, heads),
        out_shape=jax.ShapeDtypeStruct((tok, width), BF16),
        in_specs=[pl.BlockSpec(memory_space=pl.ANY)] * 4,
        out_specs=pl.BlockSpec(memory_space=pl.ANY),
        scratch_shapes=[
            pltpu.VMEM((tok, width), BF16),
            pltpu.VMEM((2, 2, tok, wide), BF16),
            pltpu.VMEM((2, 2, 8, tok), F32),
            pltpu.VMEM((2, 3, 4, wide), F32),
            pltpu.VMEM((2, 1, wide), F32),
            pltpu.VMEM((2, 1, wide), F32),
            pltpu.VMEM((2, HALO, wide), BF16),
            pltpu.VMEM((2, HALO, wide), BF16),
            pltpu.VMEM((2, HALO + rows, wide), F32),
            pltpu.VMEM((2, rows, wide), BF16),
            pltpu.VMEM((2, rows, wide), BF16),
            pltpu.VMEM((2, rows, wide), BF16),
            pltpu.VMEM((2, rows, wide), F32),
            pltpu.VMEM((2, wide, DH), BF16),
            pltpu.VMEM((2, n_chip, part, DH), BF16),
            pltpu.VMEM((2, n_chip, part, DH), BF16),
            pltpu.VMEM((2, wide, DH), BF16),
            pltpu.VMEM((2, 2, tok, wide), BF16),
            dma((5,)), dma((3,)), dma((3,)), dma((3,)), dma((3,)), dma((3,)), dma((3,)),
            dma((2,)), dma((2,)), dma((2,)), dma((2,)), dma((2,)), dma((2,)), dma((3,)), dma((3,)),
        ],
        compiler_params=pltpu.CompilerParams(
            collective_id=0, has_side_effects=True, vmem_limit_bytes=40 * 1024 * 1024
        ),
    )(activations[0], norm_gain, conv_kernels[0], out_gain)
    return handed[None]


def solution(mesh):
    placed = (P("pipe", "seq", None), P("pipe", None), P("pipe", None, None, None), P("pipe", None))
    return jax.shard_map(
        body, mesh=mesh, in_specs=placed, out_specs=P("pipe", "seq", None), check_vma=False
    )
```

time: 281 us -> 51.2 us (0.18)
  the two profiles are of different devices: /device:TPU:63 before, /device:TPU:1 now
where the time goes in v1:
time: 51.2 us; the launch traced here: 50.9 us
  Pallas kernels  46.8 us (91%)
  local copies, waits for them, and re-layouts  4.12 us (8%)
    pallas_call x1, Pallas kernels, body(): pl.pallas_call(functools.partial(kernel, n_pipe, n_chip, tok, heads), out...  46.8 us
    unnamed x9, local copies, waits for them, and re-layouts  4.12 us

profile of v1, /device:TPU:1, one launch (start us, length us, event | category | flops | bytes accessed | tf_op | source)
XLA Modules:
  0.0 50.9 jit_solution(5602725988365206845)
XLA Ops:
  0.0 0.0 copy-start
  0.0 1.0 %copy-done = bf16[1,128,2048]{2,1,0:T(8,128)(2,1)S(1)} copy-done((bf16[1,128,2048]{2,1,0:T(8,128)(2,1)S(1)}, bf16[1,128,2048]{2,1,0:T(8,128)(2,1)}, u32[]{:S(2)}) %copy-start) | copy-done | bytes 524312
  1.0 0.0 copy-start.1
  1.0 0.9 %copy-done.1 = f32[1,3,4,2048]{3,2,1,0:T(4,128)S(1)} copy-done((f32[1,3,4,2048]{3,2,1,0:T(4,128)S(1)}, f32[1,3,4,2048]{3,2,1,0:T(4,128)}, u32[]{:S(2)}) %copy-start.1) | copy-done | bytes 98328
  1.9 0.0 copy-start.2
  1.9 0.7 %copy-done.2 = f32[1,2048]{1,0:T(1,128)S(1)} copy-done((f32[1,2048]{1,0:T(1,128)S(1)}, f32[1,2048]{1,0:T(1,128)}, u32[]{:S(2)}) %copy-start.2) | copy-done | bytes 8216
  2.6 0.0 copy-start.3
  2.6 0.7 %copy-done.3 = f32[1,2048]{1,0:T(1,128)S(1)} copy-done((f32[1,2048]{1,0:T(1,128)S(1)}, f32[1,2048]{1,0:T(1,128)}, u32[]{:S(2)}) %copy-start.3) | copy-done | bytes 8216
  3.3 46.8 %shard_map.46 = bf16[128,2048]{1,0:T(8,128)(2,1)S(1)} custom-call(bf16[128,2048]{1,0:T(8,128)(2,1)S(1)} %bitcast.4, f32[1,2048]{1,0:T(1,128)S(1)} %copy-done.2, f32[3,4,2048]{2,1,0:T(4,128)S(1)} %bitcast.5, f32[1,2048]{1,0:T(1,128)S(1)} %copy-done.3), custom_call_target="tpu_custom_call" | custom-call | tf_op jit(solution)/shard_map/pallas_call | solution.py:357
  50.1 0.8 %copy.6 = bf16[1,128,2048]{2,1,0:T(8,128)(2,1)} copy(bf16[1,128,2048]{2,1,0:T(8,128)(2,1)S(1)} %bitcast.3) | data formatting | bytes 1048576
Async XLA Ops:
  0.0 1.0 %copy-start = (bf16[1,128,2048]{2,1,0:T(8,128)(2,1)S(1)}, bf16[1,128,2048]{2,1,0:T(8,128)(2,1)}, u32[]{:S(2)}) copy-start(bf16[1,128,2048]{2,1,0:T(8,128)(2,1)} %param.4) | copy-start | bytes 1572868
  1.0 0.9 %copy-start.1 = (f32[1,3,4,2048]{3,2,1,0:T(4,128)S(1)}, f32[1,3,4,2048]{3,2,1,0:T(4,128)}, u32[]{:S(2)}) copy-start(f32[1,3,4,2048]{3,2,1,0:T(4,128)} %param.6) | copy-start | bytes 294916
  1.9 0.7 %copy-start.2 = (f32[1,2048]{1,0:T(1,128)S(1)}, f32[1,2048]{1,0:T(1,128)}, u32[]{:S(2)}) copy-start(f32[1,2048]{1,0:T(1,128)} %ngain.1) | copy-start | bytes 24580
  2.6 0.7 %copy-start.3 = (f32[1,2048]{1,0:T(1,128)S(1)}, f32[1,2048]{1,0:T(1,128)}, u32[]{:S(2)}) copy-start(f32[1,2048]{1,0:T(1,128)} %ogain.1) | copy-start | bytes 24580

commit v2 on v0

v2 whole, which is shorter than its diff:
```python
import functools

import jax
import jax.numpy as jnp
from jax import lax
from jax.experimental import pallas as pl
from jax.experimental.pallas import tpu as pltpu
from jax.sharding import PartitionSpec as P

DH = 128
HALO = 16
GROUPS = 2
PIECES = 4
OWNER = (0, 0)
EARLY = 2
ROW = 8
MESH = pl.DeviceIdType.MESH
F32 = jnp.float32
BF16 = jnp.bfloat16


def lanes(start, size):
    return pl.ds(pl.multiple_of(start, DH), size)


def kernel(
    n_pipe, n_chip, n_y, tok, heads,
    act, ngain, conv, ogain, out,
    own, sx, sf, column, pconv, pngain, pogain, snb, sk, sv, hsend, chalo, rhalo,
    tsend, trecv, rsend, rrecv, psend, pbuf, rx, rf, rnb, rq, rk, rv, within, res,
    load_sem, xs, xr, fs, fr, ps, pr, hs, hr, gs, gr, zs, zr,
    ts, tr, es, er, qs, qr, os_sem, or_sem,
):
    wide = heads * DH
    rows = 2 * tok
    each = heads // GROUPS
    gwide = each * DH
    part = gwide // n_y
    n_x = n_chip // n_y
    pipe = lax.axis_index("pipe")
    seq = lax.axis_index("seq")
    core = seq % 2
    chip = seq // 2
    x_at = chip // n_y
    y_at = chip % n_y
    ahead = (pipe + 1) % n_pipe
    behind = (pipe + n_pipe - 1) % n_pipe
    peer = seq + 1 - 2 * core
    next_chip = (chip + 1) % n_chip
    last_chip = (chip + n_chip - 1) % n_chip
    y_steps = sorted(range(1, n_y), key=lambda k: -min(k, n_y - k))
    x_steps = sorted(range(1, n_x), key=lambda k: -min(k, n_x - k))

    def on_row(step):
        return (y_at + step) % n_y

    def row_seq(y):
        return 2 * (x_at * n_y + y) + core

    def column_seq(x):
        return 2 * (x * n_y + y_at) + core

    def remote(src, dst, send, recv, to_pipe, to_seq):
        return pltpu.make_async_remote_copy(
            src_ref=src, dst_ref=dst, send_sem=send, recv_sem=recv,
            device_id=(to_pipe, to_seq), device_id_type=MESH,
        )

    def greet(to_pipe, to_seq):
        pl.semaphore_signal(barrier, inc=1, device_id=(to_pipe, to_seq), device_id_type=MESH)

    pending = []

    def finished():
        for wait in pending:
            wait()

    barrier = pltpu.get_barrier_semaphore()
    greet(pipe, peer)
    for which in range(2):
        greet(behind, 2 * chip + which)
    greet(pipe, 2 * last_chip + 1)
    for step in y_steps:
        greet(pipe, row_seq(on_row(step)))
        if 1 in OWNER:
            greet(behind, row_seq(on_row(step)))
    for step in x_steps:
        greet(pipe, column_seq((x_at + step) % n_x))

    half = lanes(core * wide, wide)
    loads = [
        pltpu.make_async_copy(act, own, load_sem.at[0]),
        pltpu.make_async_copy(conv.at[:, :, half], pconv.at[0], load_sem.at[1]),
        pltpu.make_async_copy(ngain, pngain.at[0], load_sem.at[2]),
    ]
    for load in loads:
        load.start()
    for load in loads:
        load.wait()

    squares = jnp.zeros((tok, DH), F32)
    for piece in range(2 * wide // DH):
        values = own[:, piece * DH : (piece + 1) * DH].astype(F32)
        squares = squares + values * values
    mean = jnp.sum(squares, axis=-1, keepdims=True) * (1.0 / (2 * wide))
    factor = jnp.broadcast_to(lax.rsqrt(mean + 1e-06), (tok, DH))
    column[0] = factor
    sf[0] = factor.T[:8]

    def halo_rows(head, carry):
        cols = lanes(head * DH, DH)
        hsend[:, cols] = (
            own[tok - HALO :, cols].astype(F32) * column[0, tok - HALO :, :] * pngain[0, :, cols]
        ).astype(BF16)
        return carry

    lax.fori_loop(0, 2 * heads, halo_rows, 0)

    def positive(x):
        return jnp.where(x > 0.0, x + 1.0, jnp.exp(jnp.minimum(x, 0.0)))

    def convolved(ref, start, count, which, j, cols):
        total = pconv[which, j, 0:1, cols] * ref[pl.ds(HALO + start, count), cols]
        for i in range(1, 4):
            total = total + pconv[which, j, i : i + 1, cols] * ref[
                pl.ds(HALO + start - i, count), cols
            ]
        return total

    def keys_values(slot, start, count, head):
        cols = lanes(head * DH, DH)
        ref = snb.at[slot]
        where = pl.ds(slot * tok + start, count)
        sk[where, cols] = positive(convolved(ref, start, count, 0, 1, cols)).astype(BF16)
        sv[where, cols] = convolved(ref, start, count, 0, 2, cols).astype(BF16)

    def state_rows(slot, first, last):
        def one(head, carry):
            cols = lanes(head * DH, DH)
            raw = own[:, lanes(core * wide + head * DH, DH)] if slot == 0 else sx[:, cols]
            normed = (
                raw.astype(F32) * column[slot] * pngain[0, :, lanes(core * wide + head * DH, DH)]
            ).astype(BF16)
            snb[slot, HALO:, cols] = normed.astype(F32)
            keys_values(slot, HALO, tok - HALO, head)
            return carry

        lax.fori_loop(first, last, one, 0, unroll=True)

    state_rows(0, 0, heads)

    pl.semaphore_wait(barrier, 3 + (1 + (1 in OWNER)) * len(y_steps) + len(x_steps) + 2 * core)
    x_copies = [
        remote(
            act.at[:, lanes((1 - core) * wide + group * gwide, gwide)],
            sx.at[:, pl.ds(group * gwide, gwide)],
            xs.at[group], xr.at[group], pipe, peer,
        )
        for group in range(GROUPS)
    ]
    f_copies = [remote(sf.at[0], sf.at[1], fs.at[0], fr.at[0], pipe, peer)]
    for which in range(2):
        f_copies.append(
            remote(sf.at[0], rf.at[core], fs.at[1 + which], fr.at[1 + core], ahead, 2 * chip + which)
        )
    h_copies = [
        remote(
            hsend.at[:, pl.ds(which * wide, wide)], chalo,
            hs.at[which], hr, pipe, 2 * next_chip + which,
        )
        for which in range(2)
    ]
    p_copies = [
        remote(conv.at[:, :, half], pconv.at[1], ps.at[0], pr.at[0], ahead, seq),
        remote(ngain, pngain.at[1], ps.at[1], pr.at[1], ahead, seq),
        remote(ogain, pogain, ps.at[2], pr.at[2], ahead, seq),
    ]

    pwide = wide // PIECES

    def raw_copy(piece, which):
        return remote(
            act.at[:, pl.ds(which * wide + piece * pwide, pwide)],
            rx.at[core, :, pl.ds(piece * pwide, pwide)],
            zs.at[piece, which], zr.at[piece, core], ahead, 2 * chip + which,
        )

    def send_raw(first, last):
        for piece in range(first, last):
            for which in range(2):
                copy = raw_copy(piece, which)
                copy.start()
                pending.append(copy.wait_send)

    @pl.when(core == 1)
    def _():
        for copy in h_copies:
            copy.start()

    f_copies[0].start()
    for copy in x_copies:
        copy.start()
    for copy in f_copies[1:] + p_copies:
        copy.start()
    send_raw(0, EARLY)

    def wait_sent_halo():
        @pl.when(core == 1)
        def _():
            for copy in h_copies:
                copy.wait_send()

    pending.append(wait_sent_halo)
    pending.extend(copy.wait_send for copy in x_copies)
    pending.append(f_copies[0].wait_send)
    pending.extend(copy.wait_send for copy in f_copies[1:] + p_copies)

    f_copies[0].wait_recv()
    column[1] = jnp.broadcast_to(sf[1, 0:1, :], (tok, tok)).T
    g_copy = remote(chalo, rhalo, gs, gr, ahead, seq)

    def edges(group):
        cols = pl.ds(group * gwide, gwide)
        before = jnp.where(chip == 0, 0.0, chalo[:, cols].astype(F32))
        snb[0, :HALO, cols] = jnp.where(core == 0, before, snb[1, tok:, cols])
        snb[1, :HALO, cols] = jnp.where(core == 0, snb[0, tok:, cols], before)

    def t_copy(group, y):
        return remote(
            tsend.at[group, pl.ds(pl.multiple_of(y * part, part), part)],
            trecv.at[group, y_at], ts.at[group], tr.at[group],
            (pipe, ahead)[OWNER[group]], row_seq(y),
        )

    def t_all(group):
        count = n_y - 1 + OWNER[group]
        return remote(
            psend.at[group, pl.ds(0, count)], trecv.at[group, pl.ds(0, count)],
            ts.at[group], tr.at[group], pipe, peer,
        )

    def slice_of(y):
        return pl.ds(pl.multiple_of(y * part, part), part)

    for group in range(GROUPS):
        x_copies[group].wait_recv()
        state_rows(1, group * each, (group + 1) * each)
    h_copies[0].wait_recv()
    g_copy.start()
    pending.append(g_copy.wait_send)
    for group in range(GROUPS):
        edges(group)

        def one(index, carry, group=group):
            head = group * each + index
            cols = lanes(head * DH, DH)
            for slot in range(2):
                keys_values(slot, 0, HALO, head)
            state = lax.dot_general(
                sk[:, cols], sv[:, cols], (((0,), (0,)), ((), ())), preferred_element_type=F32
            )
            tsend[group, lanes(index * DH, DH), :] = state.astype(BF16)
            return carry

        lax.fori_loop(0, each, one, 0, unroll=True)
        for step in y_steps + [0] * OWNER[group]:
            t_copy(group, on_row(step)).start()
        if OWNER[group] == 0:
            trecv[group, y_at] = tsend[group, slice_of(y_at), :]
        pending.append(t_all(group).wait_send)
    send_raw(EARLY, PIECES)

    def arrived_raw(piece):
        for which in range(2):
            remote(
                sx.at[:, pl.ds(0, pwide)], rx.at[which, :, pl.ds(piece * pwide, pwide)],
                xs.at[0], zr.at[piece, which], ahead, seq,
            ).wait_recv()

    def arrived_first():
        for which in range(2):
            remote(sf.at[0], rf.at[which], fs.at[0], fr.at[1 + which], ahead, seq).wait_recv()
        for copy in p_copies:
            copy.wait_recv()
        g_copy.wait_recv()

    def e_copy(group, x):
        return remote(
            rsend.at[group], rrecv.at[group, x_at], es.at[group], er.at[group], pipe, column_seq(x)
        )

    def e_all(group):
        return remote(
            psend.at[group, pl.ds(0, n_x - 1)], rrecv.at[group, pl.ds(0, n_x - 1)],
            es.at[group], er.at[group], pipe, peer,
        )

    def q_copy(group, y):
        return remote(
            psend.at[group, y], pbuf.at[group, slice_of(y_at)],
            qs.at[group], qr.at[group], (ahead, pipe)[OWNER[group]], row_seq(y),
        )

    def q_all(group):
        count = (n_y - OWNER[group]) * part
        return remote(
            tsend.at[group, pl.ds(0, count)], pbuf.at[group, pl.ds(0, count)],
            qs.at[group], qr.at[group], ahead, seq,
        )

    def totals(group):
        t_all(group).wait_recv()
        total = trecv[group, 0].astype(F32)
        for y in range(1, n_y):
            total = total + trecv[group, y].astype(F32)
        rsend[group] = total.astype(BF16)
        for step in x_steps:
            e_copy(group, (x_at + step) % n_x).start()
        rrecv[group, x_at] = rsend[group]
        pending.append(e_all(group).wait_send)

    def prefixes(group):
        e_all(group).wait_recv()
        total = jnp.zeros((part, DH), F32)
        for x in range(n_x):
            total = total + jnp.where(x < x_at, rrecv[group, x].astype(F32), 0.0)
        for y in range(n_y):
            psend[group, y] = total.astype(BF16)
            total = total + trecv[group, y].astype(F32)
        for step in y_steps + [0] * (1 - OWNER[group]):
            q_copy(group, on_row(step)).start()
        if OWNER[group] == 1:
            pbuf[group, slice_of(y_at), :] = psend[group, y_at]
        pending.append(q_all(group).wait_send)

    def own_half(head):
        return lanes(core * wide + head * DH, DH)

    def first_of_behind():
        arrived_first()
        for block in range(2):
            column[block] = jnp.broadcast_to(rf[block, 0:1, :], (tok, tok)).T
        rnb[:HALO, :] = jnp.where(chip == 0, 0.0, rhalo[...].astype(F32))

    def inside(piece):
        arrived_raw(piece)
        tile = tok // 2
        query_at = lax.broadcasted_iota(jnp.int32, (tok, rows), 0)
        key_at = lax.broadcasted_iota(jnp.int32, (tok, rows), 1)

        def one(index, carry):
            head = piece * (heads // PIECES) + index
            cols = lanes(head * DH, DH)
            for block in range(2):
                normed = (
                    rx[block, :, cols].astype(F32) * column[block] * pngain[1, :, own_half(head)]
                ).astype(BF16)
                rnb[pl.ds(HALO + block * tok, tok), cols] = normed.astype(F32)
            for start in range(0, rows, tile):
                where = pl.ds(start, tile)
                rq[where, cols] = positive(convolved(rnb, start, tile, 1, 0, cols)).astype(BF16)
                rk[where, cols] = positive(convolved(rnb, start, tile, 1, 1, cols)).astype(BF16)
                rv[where, cols] = convolved(rnb, start, tile, 1, 2, cols).astype(BF16)
            for block in range(2):
                here, until = pl.ds(block * tok, tok), (block + 1) * tok
                scores = lax.dot_general(
                    rq[here, cols], rk[:until, cols], (((1,), (1,)), ((), ())),
                    preferred_element_type=F32,
                )
                causal = key_at[:, :until] <= query_at[:, :until] + block * tok
                weights = jnp.where(causal, scores, 0.0).astype(BF16)
                within[here, cols] = jnp.dot(
                    weights, rv[:until, cols], preferred_element_type=F32
                )
            return carry

        lax.fori_loop(0, heads // PIECES, one, 0, unroll=True)

    def o_copy(head):
        return remote(
            res.at[1 - core, :, lanes(head * DH, DH)], out.at[:, own_half(head)],
            os_sem.at[0], or_sem, pipe, peer,
        )

    def keep_copy(head):
        return pltpu.make_async_copy(
            res.at[core, :, lanes(head * DH, DH)], out.at[:, own_half(head)], os_sem.at[1]
        )

    def finish(group):
        q_all(group).wait_recv()

        def one(index, carry):
            head = group * each + index
            cols = lanes(head * DH, DH)
            mixed = within[:, cols] + jnp.dot(
                rq[:, cols], pbuf[group, lanes(index * DH, DH), :], preferred_element_type=F32
            )
            square = jnp.dot(
                (mixed * mixed).astype(BF16), jnp.full((DH, DH), 1.0 / DH, BF16),
                preferred_element_type=F32,
            )
            scaled = mixed * lax.rsqrt(square + 1e-06) * pogain[:, own_half(head)]
            for block in range(2):
                res[block, :, cols] = (
                    rx[block, :, cols].astype(F32) + scaled[block * tok : (block + 1) * tok]
                ).astype(BF16)
            o_copy(head).start()
            keep_copy(head).start()
            return carry

        lax.fori_loop(0, each, one, 0, unroll=True)

    totals(0)
    if OWNER[1] == 0:
        totals(1)
    prefixes(0)
    if OWNER[1] == 0:
        prefixes(1)
    first_of_behind()
    for piece in range(PIECES // 2):
        inside(piece)
    if OWNER[1] == 1:
        totals(1)
        prefixes(1)
    for piece in range(PIECES // 2, PIECES):
        inside(piece)
    for group in range(GROUPS):
        finish(group)

    everything = remote(
        res.at[1 - core], out.at[:, lanes((1 - core) * wide, wide)], os_sem.at[0], or_sem, pipe, peer
    )
    everything.wait_send()
    everything.wait_recv()
    pltpu.make_async_copy(res.at[core], out.at[:, half], os_sem.at[1]).wait()
    finished()


def body(activations, norm_gain, conv_kernels, out_gain):
    n_pipe = lax.axis_size("pipe")
    n_chip = lax.axis_size("seq") // 2
    n_y = min(ROW, n_chip)
    n_x = n_chip // n_y
    _, tok, width = activations.shape
    wide = width // 2
    heads = wide // DH
    gwide = wide // GROUPS
    part = gwide // n_y
    rows = 2 * tok
    dma = pltpu.SemaphoreType.DMA
    handed = pl.pallas_call(
        functools.partial(kernel, n_pipe, n_chip, n_y, tok, heads),
        out_shape=jax.ShapeDtypeStruct((tok, width), BF16),
        in_specs=[pl.BlockSpec(memory_space=pltpu.HBM)] * 4,
        out_specs=pl.BlockSpec(memory_space=pl.ANY),
        scratch_shapes=[
            pltpu.VMEM((tok, width), BF16),
            pltpu.VMEM((tok, wide), BF16),
            pltpu.VMEM((2, 8, tok), F32),
            pltpu.VMEM((2, tok, DH), F32),
            pltpu.VMEM((2, 3, 4, wide), F32),
            pltpu.VMEM((2, 1, width), F32),
            pltpu.VMEM((1, width), F32),
            pltpu.VMEM((2, HALO + tok, wide), F32),
            pltpu.VMEM((rows, wide), BF16),
            pltpu.VMEM((rows, wide), BF16),
            pltpu.VMEM((HALO, width), BF16),
            pltpu.VMEM((HALO, wide), BF16),
            pltpu.VMEM((HALO, wide), BF16),
            pltpu.VMEM((GROUPS, gwide, DH), BF16),
            pltpu.VMEM((GROUPS, n_y, part, DH), BF16),
            pltpu.VMEM((GROUPS, part, DH), BF16),
            pltpu.VMEM((GROUPS, n_x, part, DH), BF16),
            pltpu.VMEM((GROUPS, n_y, part, DH), BF16),
            pltpu.VMEM((GROUPS, gwide, DH), BF16),
            pltpu.VMEM((2, tok, wide), BF16),
            pltpu.VMEM((2, 8, tok), F32),
            pltpu.VMEM((HALO + rows, wide), F32),
            pltpu.VMEM((rows, wide), BF16),
            pltpu.VMEM((rows, wide), BF16),
            pltpu.VMEM((rows, wide), BF16),
            pltpu.VMEM((rows, wide), F32),
            pltpu.VMEM((2, tok, wide), BF16),
            dma((3,)), dma((GROUPS,)), dma((GROUPS,)), dma((3,)), dma((3,)), dma((3,)), dma((3,)), dma((2,)), dma,
            dma, dma, dma((PIECES, 2)), dma((PIECES, 2)),
            dma((GROUPS,)), dma((GROUPS,)), dma((GROUPS,)), dma((GROUPS,)),
            dma((GROUPS,)), dma((GROUPS,)), dma((2,)), dma,
        ],
        compiler_params=pltpu.CompilerParams(
            collective_id=0, has_side_effects=True, vmem_limit_bytes=60 * 1024 * 1024
        ),
    )(activations[0], norm_gain, conv_kernels[0], out_gain)
    return handed[None]


def solution(mesh):
    placed = (P("pipe", "seq", None), P("pipe", None), P("pipe", None, None, None), P("pipe", None))
    return jax.shard_map(
        body, mesh=mesh, in_specs=placed, out_specs=P("pipe", "seq", None), check_vma=False
    )
```

time: 281 us -> 42 us (0.15)
  the two profiles are of different devices: /device:TPU:63 before, /device:TPU:1 now
where the time goes in v2:
time: 42 us; the launch traced here: 41.8 us
  Pallas kernels  39.9 us (95%)
  local copies, waits for them, and re-layouts  1.88 us (4%)
    pallas_call x1, Pallas kernels, body(): pl.pallas_call(functools.partial(kernel, n_pipe, n_chip, n_y, tok, heads)...  39.9 us
    unnamed x1, local copies, waits for them, and re-layouts  1.88 us

profile of v2, /device:TPU:1, one launch (start us, length us, event | category | flops | bytes accessed | tf_op | source)
XLA Modules:
  0.0 41.8 jit_solution(10705748682882634566)
XLA Ops:
  0.0 39.9 %shard_map.46 = bf16[128,2048]{1,0:T(8,128)(2,1)} custom-call(bf16[128,2048]{1,0:T(8,128)(2,1)} %bitcast.4, f32[1,2048]{1,0:T(1,128)} %ngain.1, f32[3,4,2048]{2,1,0:T(4,128)} %bitcast.5, f32[1,2048]{1,0:T(1,128)} %ogain.1), custom_call_target="tpu_custom_call" | custom-call | tf_op jit(solution)/shard_map/pallas_call | solution.py:452
  39.9 1.9 %copy.6 = bf16[1,128,2048]{2,1,0:T(8,128)(2,1)} copy(bf16[1,128,2048]{2,1,0:T(8,128)(2,1)} %bitcast.3) | data formatting | bytes 1048576

commit v3 on v2

--- a/solution.py
+++ b/solution.py
@@ -9,10 +9,16 @@
 
 DH = 128
 HALO = 16
-GROUPS = 2
-PIECES = 4
-OWNER = (0, 0)
+GROUP_HEADS = (4, 4)
+OWNER = (0, 1)
+FIRST = 1
+TILE = 64
+SECOND = 3
+GROUPS = len(GROUP_HEADS)
+RELAY = True
+PIECES = 8
 EARLY = 2
+PAIR = 2
 ROW = 8
 MESH = pl.DeviceIdType.MESH
 F32 = jnp.float32
@@ -28,14 +34,13 @@
     act, ngain, conv, ogain, out,
     own, sx, sf, column, pconv, pngain, pogain, snb, sk, sv, hsend, chalo, rhalo,
     tsend, trecv, rsend, rrecv, psend, pbuf, rx, rf, rnb, rq, rk, rv, within, res,
-    load_sem, xs, xr, fs, fr, ps, pr, hs, hr, gs, gr, zs, zr,
+    relay, load_sem, xs, xr, fs, fr, ps, pr, hs, hr, gs, gr, zs, zr,
     ts, tr, es, er, qs, qr, os_sem, or_sem,
 ):
     wide = heads * DH
     rows = 2 * tok
-    each = heads // GROUPS
-    gwide = each * DH
-    part = gwide // n_y
+    firsts = [sum(GROUP_HEADS[:group]) for group in range(GROUPS)]
+    rows_each = DH // n_y
     n_x = n_chip // n_y
     pipe = lax.axis_index("pipe")
     seq = lax.axis_index("seq")
@@ -49,6 +54,8 @@
     next_chip = (chip + 1) % n_chip
     last_chip = (chip + n_chip - 1) % n_chip
     y_steps = sorted(range(1, n_y), key=lambda k: -min(k, n_y - k))
+    far = n_y // 2 if RELAY and n_y >= 4 else 0
+    near_steps = [step for step in y_steps if step != far]
     x_steps = sorted(range(1, n_x), key=lambda k: -min(k, n_x - k))
 
     def on_row(step):
@@ -80,12 +87,18 @@
     for which in range(2):
         greet(behind, 2 * chip + which)
     greet(pipe, 2 * last_chip + 1)
-    for step in y_steps:
+    for step in near_steps:
         greet(pipe, row_seq(on_row(step)))
-        if 1 in OWNER:
+    if 1 in OWNER:
+        for step in y_steps:
             greet(behind, row_seq(on_row(step)))
     for step in x_steps:
         greet(pipe, column_seq((x_at + step) % n_x))
+
+    @pl.when(chip == 0)
+    def _():
+        chalo[...] = jnp.zeros(chalo.shape, BF16)
+        rhalo[...] = jnp.zeros(rhalo.shape, BF16)
 
     half = lanes(core * wide, wide)
     loads = [
@@ -114,7 +127,7 @@
         ).astype(BF16)
         return carry
 
-    lax.fori_loop(0, 2 * heads, halo_rows, 0)
+    lax.fori_loop(0, 2 * heads, halo_rows, 0, unroll=True)
 
     def positive(x):
         return jnp.where(x > 0.0, x + 1.0, jnp.exp(jnp.minimum(x, 0.0)))
@@ -147,16 +160,19 @@
 
         lax.fori_loop(first, last, one, 0, unroll=True)
 
-    state_rows(0, 0, heads)
-
-    pl.semaphore_wait(barrier, 3 + (1 + (1 in OWNER)) * len(y_steps) + len(x_steps) + 2 * core)
+    pl.semaphore_wait(barrier, 3 + len(near_steps) + (1 in OWNER) * len(y_steps) + len(x_steps) + 2 * core)
+    if far:
+        pl.semaphore_signal(
+            relay, inc=1, device_id=(pipe, row_seq(on_row(n_y - 1))), device_id_type=MESH
+        )
+
     x_copies = [
         remote(
-            act.at[:, lanes((1 - core) * wide + group * gwide, gwide)],
-            sx.at[:, pl.ds(group * gwide, gwide)],
-            xs.at[group], xr.at[group], pipe, peer,
-        )
-        for group in range(GROUPS)
+            act.at[:, lanes((1 - core) * wide + chunk * (wide // 2), wide // 2)],
+            sx.at[:, pl.ds(chunk * (wide // 2), wide // 2)],
+            xs.at[chunk], xr.at[chunk], pipe, peer,
+        )
+        for chunk in range(2)
     ]
     f_copies = [remote(sf.at[0], sf.at[1], fs.at[0], fr.at[0], pipe, peer)]
     for which in range(2):
@@ -192,7 +208,9 @@
                 copy.start()
                 pending.append(copy.wait_send)
 
-    @pl.when(core == 1)
+    sends_halo = jnp.logical_and(core == 1, next_chip != 0)
+
+    @pl.when(sends_halo)
     def _():
         for copy in h_copies:
             copy.start()
@@ -205,7 +223,7 @@
     send_raw(0, EARLY)
 
     def wait_sent_halo():
-        @pl.when(core == 1)
+        @pl.when(sends_halo)
         def _():
             for copy in h_copies:
                 copy.wait_send()
@@ -215,58 +233,79 @@
     pending.append(f_copies[0].wait_send)
     pending.extend(copy.wait_send for copy in f_copies[1:] + p_copies)
 
+    state_rows(0, 0, heads)
     f_copies[0].wait_recv()
     column[1] = jnp.broadcast_to(sf[1, 0:1, :], (tok, tok)).T
-    g_copy = remote(chalo, rhalo, gs, gr, ahead, seq)
-
     def edges(group):
-        cols = pl.ds(group * gwide, gwide)
-        before = jnp.where(chip == 0, 0.0, chalo[:, cols].astype(F32))
+        cols = pl.ds(firsts[group] * DH, GROUP_HEADS[group] * DH)
+        before = chalo[:, cols].astype(F32)
         snb[0, :HALO, cols] = jnp.where(core == 0, before, snb[1, tok:, cols])
         snb[1, :HALO, cols] = jnp.where(core == 0, snb[0, tok:, cols], before)
 
+    def part(group):
+        return GROUP_HEADS[group] * rows_each
+
+    def held(group):
+        return pl.ds(firsts[group] * rows_each, part(group))
+
+    def slice_of(group, y):
+        return pl.ds(pl.multiple_of(firsts[group] * DH + y * part(group), 16), part(group))
+
     def t_copy(group, y):
         return remote(
-            tsend.at[group, pl.ds(pl.multiple_of(y * part, part), part)],
-            trecv.at[group, y_at], ts.at[group], tr.at[group],
-            (pipe, ahead)[OWNER[group]], row_seq(y),
+            tsend.at[slice_of(group, y)], trecv.at[y_at, held(group)],
+            ts.at[group], tr.at[group], (pipe, ahead)[OWNER[group]], row_seq(y),
         )
 
     def t_all(group):
         count = n_y - 1 + OWNER[group]
         return remote(
-            psend.at[group, pl.ds(0, count)], trecv.at[group, pl.ds(0, count)],
+            psend.at[pl.ds(0, count), held(group)], trecv.at[pl.ds(0, count), held(group)],
             ts.at[group], tr.at[group], pipe, peer,
         )
 
-    def slice_of(y):
-        return pl.ds(pl.multiple_of(y * part, part), part)
-
-    for group in range(GROUPS):
-        x_copies[group].wait_recv()
-        state_rows(1, group * each, (group + 1) * each)
-    h_copies[0].wait_recv()
-    g_copy.start()
-    pending.append(g_copy.wait_send)
+    for chunk in range(2):
+        x_copies[chunk].wait_recv()
+        state_rows(1, chunk * (heads // 2), (chunk + 1) * (heads // 2))
+    g_copy = remote(chalo, rhalo, gs, gr, ahead, seq)
+
+    @pl.when(chip != 0)
+    def _():
+        h_copies[0].wait_recv()
+        g_copy.start()
+
+    def wait_sent_on():
+        @pl.when(chip != 0)
+        def _():
+            g_copy.wait_send()
+
+    pending.append(wait_sent_on)
     for group in range(GROUPS):
         edges(group)
 
         def one(index, carry, group=group):
-            head = group * each + index
+            head = firsts[group] + index
             cols = lanes(head * DH, DH)
             for slot in range(2):
                 keys_values(slot, 0, HALO, head)
             state = lax.dot_general(
                 sk[:, cols], sv[:, cols], (((0,), (0,)), ((), ())), preferred_element_type=F32
             )
-            tsend[group, lanes(index * DH, DH), :] = state.astype(BF16)
+            tsend[lanes(head * DH, DH), :] = state.astype(BF16)
             return carry
 
-        lax.fori_loop(0, each, one, 0, unroll=True)
-        for step in y_steps + [0] * OWNER[group]:
-            t_copy(group, on_row(step)).start()
-        if OWNER[group] == 0:
-            trecv[group, y_at] = tsend[group, slice_of(y_at), :]
+        lax.fori_loop(0, GROUP_HEADS[group], one, 0, unroll=True)
+        if OWNER[group] == 1:
+            for step in y_steps + [0]:
+                t_copy(group, on_row(step)).start()
+        else:
+            for step in near_steps:
+                t_copy(group, on_row(step)).start()
+            if far:
+                if group == 0:
+                    pl.semaphore_wait(relay, 1)
+                t_copy(group, on_row(far)).start()
+            trecv[y_at, held(group), :] = tsend[slice_of(group, y_at), :]
         pending.append(t_all(group).wait_send)
     send_raw(EARLY, PIECES)
 
@@ -282,55 +321,57 @@
             remote(sf.at[0], rf.at[which], fs.at[0], fr.at[1 + which], ahead, seq).wait_recv()
         for copy in p_copies:
             copy.wait_recv()
-        g_copy.wait_recv()
+
+        @pl.when(chip != 0)
+        def _():
+            g_copy.wait_recv()
 
     def e_copy(group, x):
         return remote(
-            rsend.at[group], rrecv.at[group, x_at], es.at[group], er.at[group], pipe, column_seq(x)
+            rsend.at[held(group)], rrecv.at[x_at, held(group)],
+            es.at[group], er.at[group], pipe, column_seq(x),
         )
 
     def e_all(group):
         return remote(
-            psend.at[group, pl.ds(0, n_x - 1)], rrecv.at[group, pl.ds(0, n_x - 1)],
+            psend.at[pl.ds(0, n_x - 1), held(group)], rrecv.at[pl.ds(0, n_x - 1), held(group)],
             es.at[group], er.at[group], pipe, peer,
         )
 
     def q_copy(group, y):
         return remote(
-            psend.at[group, y], pbuf.at[group, slice_of(y_at)],
+            psend.at[y, held(group)], pbuf.at[slice_of(group, y_at)],
             qs.at[group], qr.at[group], (ahead, pipe)[OWNER[group]], row_seq(y),
         )
 
     def q_all(group):
-        count = (n_y - OWNER[group]) * part
-        return remote(
-            tsend.at[group, pl.ds(0, count)], pbuf.at[group, pl.ds(0, count)],
-            qs.at[group], qr.at[group], ahead, seq,
-        )
+        count = GROUP_HEADS[group] * DH - OWNER[group] * part(group)
+        where = pl.ds(firsts[group] * DH, count)
+        return remote(tsend.at[where], pbuf.at[where], qs.at[group], qr.at[group], ahead, seq)
 
     def totals(group):
         t_all(group).wait_recv()
-        total = trecv[group, 0].astype(F32)
+        total = trecv[0, held(group), :].astype(F32)
         for y in range(1, n_y):
-            total = total + trecv[group, y].astype(F32)
-        rsend[group] = total.astype(BF16)
+            total = total + trecv[y, held(group), :].astype(F32)
+        rsend[held(group), :] = total.astype(BF16)
         for step in x_steps:
             e_copy(group, (x_at + step) % n_x).start()
-        rrecv[group, x_at] = rsend[group]
+        rrecv[x_at, held(group), :] = rsend[held(group), :]
         pending.append(e_all(group).wait_send)
 
     def prefixes(group):
         e_all(group).wait_recv()
-        total = jnp.zeros((part, DH), F32)
+        total = jnp.zeros((part(group), DH), F32)
         for x in range(n_x):
-            total = total + jnp.where(x < x_at, rrecv[group, x].astype(F32), 0.0)
+            total = total + jnp.where(x < x_at, rrecv[x, held(group), :].astype(F32), 0.0)
         for y in range(n_y):
-            psend[group, y] = total.astype(BF16)
-            total = total + trecv[group, y].astype(F32)
+            psend[y, held(group), :] = total.astype(BF16)
+            total = total + trecv[y, held(group), :].astype(F32)
         for step in y_steps + [0] * (1 - OWNER[group]):
             q_copy(group, on_row(step)).start()
         if OWNER[group] == 1:
-            pbuf[group, slice_of(y_at), :] = psend[group, y_at]
+            pbuf[slice_of(group, y_at), :] = psend[y_at, held(group), :]
         pending.append(q_all(group).wait_send)
 
     def own_half(head):
@@ -340,11 +381,11 @@
         arrived_first()
         for block in range(2):
             column[block] = jnp.broadcast_to(rf[block, 0:1, :], (tok, tok)).T
-        rnb[:HALO, :] = jnp.where(chip == 0, 0.0, rhalo[...].astype(F32))
+        rnb[:HALO, :] = rhalo[...].astype(F32)
 
     def inside(piece):
         arrived_raw(piece)
-        tile = tok // 2
+        tile = TILE
         query_at = lax.broadcasted_iota(jnp.int32, (tok, rows), 0)
         key_at = lax.broadcasted_iota(jnp.int32, (tok, rows), 1)
 
@@ -376,55 +417,67 @@
 
         lax.fori_loop(0, heads // PIECES, one, 0, unroll=True)
 
-    def o_copy(head):
-        return remote(
-            res.at[1 - core, :, lanes(head * DH, DH)], out.at[:, own_half(head)],
+    def o_copy(first, count):
+        cols = lanes(core * wide + first * DH, count * DH)
+        return remote(
+            res.at[1 - core, :, pl.ds(first * DH, count * DH)], out.at[:, cols],
             os_sem.at[0], or_sem, pipe, peer,
         )
 
-    def keep_copy(head):
+    def keep_copy(first, count):
+        cols = lanes(core * wide + first * DH, count * DH)
         return pltpu.make_async_copy(
-            res.at[core, :, lanes(head * DH, DH)], out.at[:, own_half(head)], os_sem.at[1]
+            res.at[core, :, pl.ds(first * DH, count * DH)], out.at[:, cols], os_sem.at[1]
         )
 
     def finish(group):
         q_all(group).wait_recv()
-
-        def one(index, carry):
-            head = group * each + index
-            cols = lanes(head * DH, DH)
-            mixed = within[:, cols] + jnp.dot(
-                rq[:, cols], pbuf[group, lanes(index * DH, DH), :], preferred_element_type=F32
-            )
-            square = jnp.dot(
-                (mixed * mixed).astype(BF16), jnp.full((DH, DH), 1.0 / DH, BF16),
-                preferred_element_type=F32,
-            )
-            scaled = mixed * lax.rsqrt(square + 1e-06) * pogain[:, own_half(head)]
-            for block in range(2):
-                res[block, :, cols] = (
-                    rx[block, :, cols].astype(F32) + scaled[block * tok : (block + 1) * tok]
-                ).astype(BF16)
-            o_copy(head).start()
-            keep_copy(head).start()
-            return carry
-
-        lax.fori_loop(0, each, one, 0, unroll=True)
-
-    totals(0)
-    if OWNER[1] == 0:
+        average = jnp.full((DH, DH), 1.0 / DH, BF16)
+
+        for pair in range(GROUP_HEADS[group] // PAIR):
+            first = firsts[group] + PAIR * pair
+            mixed = []
+            for head in range(first, first + PAIR):
+                cols = lanes(head * DH, DH)
+                mixed.append(
+                    within[:, cols]
+                    + jnp.dot(rq[:, cols], pbuf[cols, :], preferred_element_type=F32)
+                )
+            squares = [
+                jnp.dot((m * m).astype(BF16), average, preferred_element_type=F32) for m in mixed
+            ]
+            for k in range(PAIR):
+                cols = lanes((first + k) * DH, DH)
+                scaled = (
+                    mixed[k] * lax.rsqrt(squares[k] + 1e-06) * pogain[:, own_half(first + k)]
+                )
+                for block in range(2):
+                    res[block, :, cols] = (
+                        rx[block, :, cols].astype(F32) + scaled[block * tok : (block + 1) * tok]
+                    ).astype(BF16)
+            o_copy(first, PAIR).start()
+            keep_copy(first, PAIR).start()
+
+    if OWNER[-1] == 0:
+        for group in range(GROUPS):
+            totals(group)
+        for group in range(GROUPS):
+            prefixes(group)
+        first_of_behind()
+        for piece in range(PIECES):
+            inside(piece)
+    else:
+        totals(0)
+        prefixes(0)
+        first_of_behind()
+        for piece in range(FIRST):
+            inside(piece)
         totals(1)
-    prefixes(0)
-    if OWNER[1] == 0:
+        for piece in range(FIRST, SECOND):
+            inside(piece)
         prefixes(1)
-    first_of_behind()
-    for piece in range(PIECES // 2):
-        inside(piece)
-    if OWNER[1] == 1:
-        totals(1)
-        prefixes(1)
-    for piece in range(PIECES // 2, PIECES):
-        inside(piece)
+        for piece in range(SECOND, PIECES):
+            inside(piece)
     for group in range(GROUPS):
         finish(group)
 
@@ -445,13 +498,12 @@
     _, tok, width = activations.shape
     wide = width // 2
     heads = wide // DH
-    gwide = wide // GROUPS
-    part = gwide // n_y
+    held = wide // n_y
     rows = 2 * tok
     dma = pltpu.SemaphoreType.DMA
     handed = pl.pallas_call(
         functools.partial(kernel, n_pipe, n_chip, n_y, tok, heads),
-        out_shape=jax.ShapeDtypeStruct((tok, width), BF16),
+        out_shape=pltpu.VMEM((tok, width), BF16),
         in_specs=[pl.BlockSpec(memory_space=pltpu.HBM)] * 4,
         out_specs=pl.BlockSpec(memory_space=pl.ANY),
         scratch_shapes=[
@@ -468,12 +520,12 @@
             pltpu.VMEM((HALO, width), BF16),
             pltpu.VMEM((HALO, wide), BF16),
             pltpu.VMEM((HALO, wide), BF16),
-            pltpu.VMEM((GROUPS, gwide, DH), BF16),
-            pltpu.VMEM((GROUPS, n_y, part, DH), BF16),
-            pltpu.VMEM((GROUPS, part, DH), BF16),
-            pltpu.VMEM((GROUPS, n_x, part, DH), BF16),
-            pltpu.VMEM((GROUPS, n_y, part, DH), BF16),
-            pltpu.VMEM((GROUPS, gwide, DH), BF16),
+            pltpu.VMEM((wide, DH), BF16),
+            pltpu.VMEM((n_y, held, DH), BF16),
+            pltpu.VMEM((held, DH), BF16),
+            pltpu.VMEM((n_x, held, DH), BF16),
+            pltpu.VMEM((n_y, held, DH), BF16),
+            pltpu.VMEM((wide, DH), BF16),
             pltpu.VMEM((2, tok, wide), BF16),
             pltpu.VMEM((2, 8, tok), F32),
             pltpu.VMEM((HALO + rows, wide), F32),
@@ -482,7 +534,7 @@
             pltpu.VMEM((rows, wide), BF16),
             pltpu.VMEM((rows, wide), F32),
             pltpu.VMEM((2, tok, wide), BF16),
-            dma((3,)), dma((GROUPS,)), dma((GROUPS,)), dma((3,)), dma((3,)), dma((3,)), dma((3,)), dma((2,)), dma,
+            pltpu.SemaphoreType.REGULAR, dma((3,)), dma((2,)), dma((2,)), dma((3,)), dma((3,)), dma((3,)), dma((3,)), dma((2,)), dma,
             dma, dma, dma((PIECES, 2)), dma((PIECES, 2)),
             dma((GROUPS,)), dma((GROUPS,)), dma((GROUPS,)), dma((GROUPS,)),
             dma((GROUPS,)), dma((GROUPS,)), dma((2,)), dma,

time: 42 us -> 40 us (0.952)
  local copies, waits for them, and re-layouts: 1.88 us -> 0.8 us
  Pallas kernels: 39.9 us -> 39.1 us
    unnamed x1, local copies, waits for them, and re-layouts: 1.88 us -> 0.8 us
    pallas_call x1, Pallas kernels: 39.9 us -> 39.1 us  [body(): pl.pallas_call(functools.partial(kernel, n_pipe, n_chip, n_y, tok, heads)...]
where the time goes in v3:
time: 40 us; the launch traced here: 39.9 us
  Pallas kernels  39.1 us (98%)
  local copies, waits for them, and re-layouts  0.8 us (2%)
    pallas_call x1, Pallas kernels, body(): pl.pallas_call(functools.partial(kernel, n_pipe, n_chip, n_y, tok, heads)...  39.1 us

profile of v3, /device:TPU:1, one launch (start us, length us, event | category | flops | bytes accessed | tf_op | source)
XLA Modules:
  0.0 39.9 jit_solution(12554453920867610197)
XLA Ops:
  0.0 39.1 %shard_map.46 = bf16[128,2048]{1,0:T(8,128)(2,1)S(1)} custom-call(bf16[128,2048]{1,0:T(8,128)(2,1)} %bitcast.4, f32[1,2048]{1,0:T(1,128)} %ngain.1, f32[3,4,2048]{2,1,0:T(4,128)} %bitcast.5, f32[1,2048]{1,0:T(1,128)} %ogain.1), custom_call_target="tpu_custom_call" | custom-call | tf_op jit(solution)/shard_map/pallas_call | solution.py:504
  39.1 0.8 %copy.6 = bf16[1,128,2048]{2,1,0:T(8,128)(2,1)} copy(bf16[1,128,2048]{2,1,0:T(8,128)(2,1)S(1)} %bitcast.3) | data formatting | bytes 1048576

commit v4 on v3

--- a/solution.py
+++ b/solution.py
@@ -15,7 +15,7 @@
 TILE = 64
 SECOND = 3
 GROUPS = len(GROUP_HEADS)
-RELAY = True
+RELAY = False
 PIECES = 8
 EARLY = 2
 PAIR = 2
@@ -188,8 +188,8 @@
     ]
     p_copies = [
         remote(conv.at[:, :, half], pconv.at[1], ps.at[0], pr.at[0], ahead, seq),
-        remote(ngain, pngain.at[1], ps.at[1], pr.at[1], ahead, seq),
-        remote(ogain, pogain, ps.at[2], pr.at[2], ahead, seq),
+        remote(ngain.at[:, half], pngain.at[1, :, half], ps.at[1], pr.at[1], ahead, seq),
+        remote(ogain.at[:, half], pogain.at[:, half], ps.at[2], pr.at[2], ahead, seq),
     ]
 
     pwide = wide // PIECES

time: 40 us -> 39.8 us (level)
  no operation moved by 1% of the time
where the time goes in v4:
time: 39.8 us; the launch traced here: 39.7 us
  Pallas kernels  38.8 us (97%)
  local copies, waits for them, and re-layouts  0.8 us (2%)
    pallas_call x1, Pallas kernels, body(): pl.pallas_call(functools.partial(kernel, n_pipe, n_chip, n_y, tok, heads)...  38.8 us

profile of v4, /device:TPU:1, one launch (start us, length us, event | category | flops | bytes accessed | tf_op | source)
XLA Modules:
  0.0 39.7 jit_solution(3459533138260758722)
XLA Ops:
  0.0 38.8 %shard_map.46 = bf16[128,2048]{1,0:T(8,128)(2,1)S(1)} custom-call(bf16[128,2048]{1,0:T(8,128)(2,1)} %bitcast.4, f32[1,2048]{1,0:T(1,128)} %ngain.1, f32[3,4,2048]{2,1,0:T(4,128)} %bitcast.5, f32[1,2048]{1,0:T(1,128)} %ogain.1), custom_call_target="tpu_custom_call" | custom-call | tf_op jit(solution)/shard_map/pallas_call | solution.py:504
  38.9 0.8 %copy.6 = bf16[1,128,2048]{2,1,0:T(8,128)(2,1)} copy(bf16[1,128,2048]{2,1,0:T(8,128)(2,1)S(1)} %bitcast.3) | data formatting | bytes 1048576
